TPU v7x, 32 devices: a whole 2x2x4 slice. The times are simulated.
32 devices in a mesh: row: 8 (over y, x, core), col: 4 (over z).
Axes of the slice: x: 2, y: 2, z: 4, core: 2. Of those that a mesh axis runs over, the one named last changes fastest.
Arguments:
- tokens: bfloat16 [8192, 2048], P('row', 'col'), may hold values from -6 to 6
- heads_weight: bfloat16 [3, 2048, 2048], P(None, 'row', 'col'), may hold values from -0.125 to 0.125
- merge_weight: bfloat16 [2048, 2048], P('row', 'col'), may hold values from -4 to 4
- expand_weight: bfloat16 [2, 2048, 8192], P(None, 'row', 'col'), may hold values from -0.125 to 0.125
- shrink_weight: bfloat16 [8192, 2048], P('row', 'col'), may hold values from -0.0625 to 0.0625
- first_gain: float32 [2048], P('col'), may hold values from 0.5 to 1.5
- second_gain: float32 [2048], P('col'), may hold values from 0.5 to 1.5
- cotangent: bfloat16 [8192, 2048], P('row', 'col'), may hold values from -10 to 10
Outputs:
- layer_output: bfloat16 [8192, 2048], P('row', 'col')
- tokens_grad: float32 [8192, 2048], P('row', 'col')
- heads_grad: float32 [3, 2048, 2048], P(None, 'row', 'col')
- merge_grad: float32 [2048, 2048], P('row', 'col')
- expand_grad: float32 [2, 2048, 8192], P(None, 'row', 'col')
- shrink_grad: float32 [8192, 2048], P('row', 'col')
- first_gain_grad: float32 [2048], P('col')
- second_gain_grad: float32 [2048], P('col')
All inputs are finite; a program needn't handle non-finite values.
Results may differ from a plain program's by a relative error of at most 0.012.
The roundings to bfloat16 on the way count: a program that leaves them out, or rounds other values in their place, can miss the bound.
Values may be sent and summed in bfloat16 or wider, within the bound.
A program may use at most 256 MiB of HBM per device.

v0:
```python
import math

import jax
import jax.numpy as jnp
from jax import lax
from jax.sharding import PartitionSpec as P

HEAD_DIM = 64


EPSILON = 1e-05
ROPE_BASE = 130000.0


def rotary_tables(length):
    position = jnp.arange(length, dtype=jnp.float32)
    inverse = jnp.power(ROPE_BASE, -jnp.arange(0, HEAD_DIM, 2, dtype=jnp.float32) / HEAD_DIM)
    angles = position[:, None] * inverse[None, :]
    angles = jnp.concatenate([angles, angles], axis=1)
    return (jnp.cos(angles), jnp.sin(angles))


def rotate(values, cosine, sine):
    half = HEAD_DIM // 2
    turned = jnp.concatenate([-values[..., half:], values[..., :half]], axis=-1)
    return values * cosine[:, None, :] + turned * sine[:, None, :]


def rotate_back(upstream, cosine, sine):
    half = HEAD_DIM // 2
    spun = upstream * sine[:, None, :]
    turned = jnp.concatenate([spun[..., half:], -spun[..., :half]], axis=-1)
    return upstream * cosine[:, None, :] + turned


def contract_rows(left, right):
    return lax.dot_general(
        left, right, (((0,), (0,)), ((), ())), preferred_element_type=jnp.float32
    )


def contract_last(left, right):
    return lax.dot_general(
        left, right, (((1,), (1,)), ((), ())), preferred_element_type=jnp.float32
    )


def row_total(values):
    return lax.psum(values, "col")


def spread(values):
    return lax.all_gather(values, "col", axis=1, tiled=True)


def collect(values):
    return lax.psum_scatter(values, "col", scatter_dimension=1, tiled=True)


def normalize(stream, gain, width):
    squares = row_total(jnp.sum(stream * stream, axis=1))
    inverse = lax.rsqrt(squares[:, None] / width + EPSILON)
    return (inverse, (stream * inverse * gain).astype(jnp.bfloat16))


def norm_back(stream, inverse, gain, upstream, width):
    weighted = gain * upstream
    inner = row_total(jnp.sum(weighted * stream, axis=1))[:, None]
    result = inverse * weighted - inverse * inverse * inverse / width * stream * inner
    gain_part = jnp.sum(upstream * (stream * inverse), axis=0)
    return (result, gain_part)


def block_scores(part, keyset, offset, block, length, factor):
    scores = jnp.einsum("qhd,khd->hqk", part, keyset, preferred_element_type=jnp.float32) * factor
    causal = (offset + jnp.arange(block))[:, None] >= jnp.arange(length)[None, :]
    return jnp.where(causal[None], scores, -1e30)


def attention_forward(queries, keyset, valueset, block):
    length = queries.shape[0]
    factor = 1.0 / math.sqrt(HEAD_DIM)
    outputs = []
    totals = []
    for offset in range(0, length, block):
        scores = block_scores(
            queries[offset : offset + block], keyset, offset, block, length, factor
        )
        peak = jnp.max(scores, axis=-1, keepdims=True)
        raised = jnp.exp(scores - peak)
        sums = jnp.sum(raised, axis=-1, keepdims=True)
        chances = raised / sums
        outputs.append(
            jnp.einsum(
                "hqk,khd->qhd",
                chances.astype(jnp.bfloat16),
                valueset,
                preferred_element_type=jnp.float32,
            )
        )
        totals.append(peak + jnp.log(sums))
    return (jnp.concatenate(outputs, axis=0), jnp.concatenate(totals, axis=1))


def attention_backward(queries, keyset, valueset, upstream, totals, block):
    length = queries.shape[0]
    factor = 1.0 / math.sqrt(HEAD_DIM)
    query_grads = []
    key_grad = jnp.zeros(keyset.shape, jnp.float32)
    value_grad = jnp.zeros(valueset.shape, jnp.float32)
    for offset in range(0, length, block):
        part = queries[offset : offset + block]
        upper = upstream[offset : offset + block]
        scores = block_scores(part, keyset, offset, block, length, factor)
        chances = jnp.exp(scores - totals[:, offset : offset + block])
        value_grad = value_grad + jnp.einsum(
            "hqk,qhd->khd", chances.astype(jnp.bfloat16), upper, preferred_element_type=jnp.float32
        )
        chance_grad = jnp.einsum(
            "qhd,khd->hqk", upper, valueset, preferred_element_type=jnp.float32
        )
        inner = jnp.sum(chances * chance_grad, axis=-1, keepdims=True)
        score_grad = (chances * (chance_grad - inner)).astype(jnp.bfloat16)
        query_grads.append(
            jnp.einsum("hqk,khd->qhd", score_grad, keyset, preferred_element_type=jnp.float32)
            * factor
        )
        key_grad = (
            key_grad
            + jnp.einsum("hqk,qhd->khd", score_grad, part, preferred_element_type=jnp.float32)
            * factor
        )
    return (jnp.concatenate(query_grads, axis=0), key_grad, value_grad)


def local(
    tokens,
    heads_weight,
    merge_weight,
    expand_weight,
    shrink_weight,
    first_gain,
    second_gain,
    cotangent,
):
    length, local_width = tokens.shape
    width = local_width * lax.axis_size("col")
    local_heads = local_width // HEAD_DIM
    block = min(512, length)
    split_shape = (length, local_heads, HEAD_DIM)
    heads_full, merge_full, expand_full, shrink_full = (
        lax.all_gather(heads_weight, "row", axis=1, tiled=True),
        lax.all_gather(merge_weight, "row", axis=0, tiled=True),
        lax.all_gather(expand_weight, "row", axis=1, tiled=True),
        lax.all_gather(shrink_weight, "row", axis=0, tiled=True),
    )
    stream = tokens.astype(jnp.float32)
    first_inverse, first_local = normalize(stream, first_gain, width)
    first_normed = spread(first_local)
    projected = jnp.einsum(
        "td,pde->pte", first_normed, heads_full, preferred_element_type=jnp.float32
    )
    cosine, sine = rotary_tables(length)
    queries = rotate(projected[0].reshape(split_shape), cosine, sine).astype(jnp.bfloat16)
    keyset = rotate(projected[1].reshape(split_shape), cosine, sine).astype(jnp.bfloat16)
    valueset = projected[2].reshape(split_shape).astype(jnp.bfloat16)
    attended, totals = attention_forward(queries, keyset, valueset, block)
    mixed = spread(attended.reshape(length, local_width).astype(jnp.bfloat16))
    middle = stream + jnp.dot(mixed, merge_full, preferred_element_type=jnp.float32)
    second_inverse, second_local = normalize(middle, second_gain, width)
    second_normed = spread(second_local)
    gate_up = jnp.einsum(
        "td,pdf->ptf", second_normed, expand_full, preferred_element_type=jnp.float32
    )
    gate = gate_up[0]
    upward = gate_up[1]
    sigmoid_gate = jax.nn.sigmoid(gate)
    activated = gate * sigmoid_gate
    hidden_local = (activated * upward).astype(jnp.bfloat16)
    upstream = cotangent.astype(jnp.float32)
    hidden = lax.all_gather(hidden_local, "col", axis=1, tiled=True)
    layer_output = (
        middle + jnp.dot(hidden, shrink_full, preferred_element_type=jnp.float32)
    ).astype(jnp.bfloat16)
    hidden_grad = lax.psum_scatter(
        contract_last(cotangent, shrink_full), "col", scatter_dimension=1, tiled=True
    )
    shrink_grad = contract_rows(hidden, cotangent)
    gate_grad = hidden_grad * upward * sigmoid_gate * (1.0 + gate * (1.0 - sigmoid_gate))
    upward_grad = hidden_grad * activated
    expand_upstream = jnp.stack([gate_grad, upward_grad]).astype(jnp.bfloat16)
    second_full = jnp.einsum(
        "ptf,pdf->td", expand_upstream, expand_full, preferred_element_type=jnp.float32
    )
    expand_grad = jnp.einsum(
        "td,ptf->pdf", second_normed, expand_upstream, preferred_element_type=jnp.float32
    )
    second_grad = collect(second_full)
    middle_part, second_gain_part = norm_back(
        middle, second_inverse, second_gain, second_grad, width
    )
    middle_grad = upstream + middle_part
    middle_low = middle_grad.astype(jnp.bfloat16)
    merge_grad = contract_rows(mixed, middle_low)
    mixed_grad = (
        collect(contract_last(middle_low, merge_full)).astype(jnp.bfloat16).reshape(split_shape)
    )
    query_grad, key_grad, value_grad = attention_backward(
        queries, keyset, valueset, mixed_grad, totals, block
    )
    heads_upstream = jnp.stack(
        [
            rotate_back(query_grad, cosine, sine).reshape(length, local_width),
            rotate_back(key_grad, cosine, sine).reshape(length, local_width),
            value_grad.reshape(length, local_width),
        ]
    ).astype(jnp.bfloat16)
    first_grad = collect(
        jnp.einsum("pte,pde->td", heads_upstream, heads_full, preferred_element_type=jnp.float32)
    )
    heads_grad = jnp.einsum(
        "td,pte->pde", first_normed, heads_upstream, preferred_element_type=jnp.float32
    )
    tokens_part, first_gain_part = norm_back(stream, first_inverse, first_gain, first_grad, width)
    tokens_grad = middle_grad + tokens_part
    heads_sum, merge_sum, expand_sum, shrink_sum = (
        lax.psum_scatter(heads_grad, "row", scatter_dimension=1, tiled=True),
        lax.psum_scatter(merge_grad, "row", scatter_dimension=0, tiled=True),
        lax.psum_scatter(expand_grad, "row", scatter_dimension=1, tiled=True),
        lax.psum_scatter(shrink_grad, "row", scatter_dimension=0, tiled=True),
    )
    first_total, second_total = lax.psum((first_gain_part, second_gain_part), "row")
    return (
        layer_output,
        tokens_grad,
        heads_sum,
        merge_sum,
        expand_sum,
        shrink_sum,
        first_total,
        second_total,
    )


def solution(mesh):
    in_specs = (
        P("row", "col"),
        P(None, "row", "col"),
        P("row", "col"),
        P(None, "row", "col"),
        P("row", "col"),
        P("col"),
        P("col"),
        P("row", "col"),
    )
    out_specs = (
        P("row", "col"),
        P("row", "col"),
        P(None, "row", "col"),
        P("row", "col"),
        P(None, "row", "col"),
        P("row", "col"),
        P("col"),
        P("col"),
    )
    return jax.shard_map(local, mesh=mesh, in_specs=in_specs, out_specs=out_specs, check_vma=False)
```

profile of v0, /device:TPU:0, one launch (start us, length us, event | category | flops | bytes accessed | tf_op | source)
XLA Modules:
  0.0 2327.8 jit_solution(8893133790210298000)
XLA Ops:
  8.8 13.5 psum.42
  23.5 2.5 fusion.27
  30.4 74.8 %all-gather.9.cloned.1.call-done = bf16[1024,2048]{1,0:T(8,128)(2,1)} async-done(((bf16[1024,512]{1,0:T(8,128)(2,1)}), bf16[1024,2048]{1,0:T(8,128)(2,1)}) %all-gather.9.cloned.1.call-update) | async-done | bytes 4194320 | tf_op jit(solution)/shard_map/all_gather | solution.py:53
  105.1 47.7 %all-gather.11.cloned.1.call-done = bf16[3,2048,512]{1,2,0:T(8,128)(2,1)} async-done(((bf16[3,256,512]{1,2,0:T(8,128)(2,1)}), bf16[3,2048,512]{1,2,0:T(8,128)(2,1)}) %all-gather.11.cloned.1.call-update) | async-done | bytes 6291472 | tf_op jit(solution)/shard_map/all_gather | solution.py:152
  152.8 10.1 fusion.22
  165.1 3.1 fusion.69
  168.2 3.5 fusion
  171.8 2.3 copy-done
  174.3 4.0 fusion.45
  178.3 3.1 fusion.68
  181.4 3.5 fusion.1
  185.0 2.2 copy-done.1
  187.2 3.8 fusion.46
  192.8 80.2 %all-gather.13.cloned.1.call-done = bf16[1024,2048]{0,1:T(8,128)(2,1)} async-done(((bf16[1024,512]{0,1:T(8,128)(2,1)}), bf16[1024,2048]{0,1:T(8,128)(2,1)}) %all-gather.13.cloned.1.call-update) | async-done | bytes 4194320 | tf_op jit(solution)/shard_map/all_gather | solution.py:53
  273.1 5.3 multiply_reduce_fusion.4
  278.4 9.2 psum.43
  289.7 38.1 %all-gather.23.cloned.1.call-done = bf16[8192,512]{1,0:T(8,128)(2,1)} async-done(((bf16[1024,512]{1,0:T(8,128)(2,1)}), bf16[8192,512]{1,0:T(8,128)(2,1)}) %all-gather.23.cloned.1.call-update) | async-done | bytes 8388624 | tf_op jit(solution)/shard_map/all_gather | solution.py:155
  327.8 18.4 fusion.70
  346.2 64.4 %all-gather.17.cloned.1.call-done = bf16[1024,2048]{1,0:T(8,128)(2,1)} async-done(((bf16[1024,512]{1,0:T(8,128)(2,1)}), bf16[1024,2048]{1,0:T(8,128)(2,1)}) %all-gather.17.cloned.1.call-update) | async-done | bytes 4194320 | tf_op jit(solution)/shard_map/all_gather | solution.py:53
  410.6 90.3 %all-gather.19.cloned.1.call-done = bf16[2,2048,2048]{2,1,0:T(8,128)(2,1)} async-done(((bf16[2,256,2048]{2,1,0:T(8,128)(2,1)}), bf16[2,2048,2048]{2,1,0:T(8,128)(2,1)}) %all-gather.19.cloned.1.call-update) | async-done | bytes 16777232 | tf_op jit(solution)/shard_map/all_gather | solution.py:154
  500.9 23.7 %convolution_bitcast_fusion.1 = f32[2,1024,2048]{2,1,0:T(8,128)} fusion(bf16[2,2048,2048]{2,1,0:T(8,128)(2,1)} %all-gather.19.cloned.1.call-done, bf16[1024,2048]{1,0:T(8,128)(2,1)} %all-gather.17.cloned.1.call-done), kind=kOutput, calls=%fused_computation.31 | convolution fusion | flops 17179869184 | bytes 37748736 | tf_op jit(solution)/shard_map/td,pdf->ptf/dot_general | solution.py:172
  524.6 530.8 %reduce-scatter.9.cloned.1.call-done = f32[1024,2048]{1,0:T(8,128)} async-done(((f32[1024,8192]{1,0:T(8,128)}), f32[1024,2048]{1,0:T(8,128)}) %reduce-scatter.9.cloned.1.call-update) | async-done | bytes 8388624 | tf_op jit(solution)/shard_map/reduce_scatter | solution.py:185
  1055.3 12.5 fusion.21
  1067.9 2.0 copy-done.20
  1071.2 21.7 fusion.14
  1093.0 145.3 %reduce-scatter.11.cloned.1.call-done = f32[1024,512]{1,0:T(8,128)} async-done(((f32[1024,2048]{1,0:T(8,128)}), f32[1024,512]{1,0:T(8,128)}) %reduce-scatter.11.cloned.1.call-update) | async-done | bytes 2097168 | tf_op jit(solution)/shard_map/reduce_scatter | solution.py:57
  1238.3 2.7 multiply_reduce_fusion.2
  1241.1 11.4 psum.44
  1252.5 2.3 subtract_add_fusion
  1256.1 5.7 fusion.49
  1262.6 25.5 %convolution_bitcast_fusion = f32[2,2048,2048]{1,2,0:T(8,128)} fusion(bf16[1,1024,2048]{2,1,0:T(8,128)(2,1)} %copy-done.21, bf16[1,1024,2048]{2,1,0:T(8,128)(2,1)} %copy-done.20, bf16[1024,2048]{1,0:T(8,128)(2,1)} %all-gather.17.cloned.1.call-done), kind=kOutput, calls=%fused_computation.14 | convolution fusion | flops 17184063488 | bytes 46137344 | tf_op jit(solution)/shard_map/td,ptf->pdf/dot_general | solution.py:195
  1289.3 1.9 copy.39
  1291.9 113.0 %reduce-scatter.13.cloned.1.call-done = f32[1024,512]{1,0:T(8,128)} async-done(((f32[1024,2048]{1,0:T(8,128)}), f32[1024,512]{1,0:T(8,128)}) %reduce-scatter.13.cloned.1.call-update) | async-done | bytes 2097168 | tf_op jit(solution)/shard_map/reduce_scatter | solution.py:57
  1407.9 16.1 multiply_reduce_fusion.1
  1425.7 8.2 multiply_convert_fusion.1
  1437.2 14.9 multiply_reduce_fusion
  1454.3 8.0 multiply_convert_fusion
  1462.2 4.9 bitcast_multiply_fusion
  1467.8 1.8 copy-done.5
  1470.1 2.7 convolution_multiply_fusion.1
  1473.6 2.7 convolution_multiply_fusion
  1479.8 2.9 copy.40
  1485.4 2.3 copy.41
  1487.7 7.3 fusion.4
  1495.0 8.8 add_convert_fusion
  1503.8 2.3 copy.42
  1506.0 3.0 fusion.39
  1509.0 11.1 convolution_bitcast_fusion.3
  1521.6 12.1 convolution_bitcast_fusion.2
  1535.4 6.5 fusion.47
  1541.9 152.7 %all-gather.21.cloned.1.call-done = bf16[1024,8192]{1,0:T(8,128)(2,1)} async-done(((bf16[1024,2048]{1,0:T(8,128)(2,1)}), bf16[1024,8192]{1,0:T(8,128)(2,1)}) %all-gather.21.cloned.1.call-update) | async-done | bytes 16777232 | tf_op jit(solution)/shard_map/all_gather | solution.py:181
  1694.6 17.2 fusion.71
  1711.9 19.0 add_convert_fusion.1
  1730.9 171.0 %reduce-scatter.21.cloned.1.call-done = f32[2,256,2048]{1,2,0:T(8,128)} async-done(((f32[2,2048,2048]{1,2,0:T(8,128)}), f32[2,256,2048]{1,2,0:T(8,128)}) %reduce-scatter.21.cloned.1.call-update) | async-done | bytes 4194320 | tf_op jit(solution)/shard_map/reduce_scatter | solution.py:229
  1901.9 5.3 copy.47
  1907.3 141.5 %reduce-scatter.15.cloned.1.call-done = f32[1024,512]{1,0:T(8,128)} async-done(((f32[1024,2048]{1,0:T(8,128)}), f32[1024,512]{1,0:T(8,128)}) %reduce-scatter.15.cloned.1.call-update) | async-done | bytes 2097168 | tf_op jit(solution)/shard_map/reduce_scatter | solution.py:57
  2048.8 2.4 fusion.28
  2051.2 14.0 all-reduce
  2065.2 11.6 psum.45
  2076.8 3.5 fusion.32
  2080.3 65.0 %reduce-scatter.17.cloned.1.call-done = f32[3,256,512]{1,2,0:T(8,128)} async-done(((f32[3,2048,512]{1,2,0:T(8,128)}), f32[3,256,512]{1,2,0:T(8,128)}) %reduce-scatter.17.cloned.1.call-update) | async-done | bytes 1572880 | tf_op jit(solution)/shard_map/reduce_scatter | solution.py:227
  2145.3 3.0 copy.46
  2148.3 52.1 %reduce-scatter.19.cloned.1.call-done = f32[256,512]{1,0:T(8,128)} async-done(((f32[2048,512]{1,0:T(8,128)}), f32[256,512]{1,0:T(8,128)}) %reduce-scatter.19.cloned.1.call-update) | async-done | bytes 524304 | tf_op jit(solution)/shard_map/reduce_scatter | solution.py:228
  2200.4 120.4 %reduce-scatter.23.cloned.1.call-done = f32[1024,512]{1,0:T(8,128)} async-done(((f32[8192,512]{1,0:T(8,128)}), f32[1024,512]{1,0:T(8,128)}) %reduce-scatter.23.cloned.1.call-update) | async-done | bytes 2097168 | tf_op jit(solution)/shard_map/reduce_scatter | solution.py:230
  (178 shorter events, 40.3 us)
Async XLA Ops:
  7.2 18.9 copy-start.34
  7.2 97.9 %all-gather.9.cloned.1.call-start = ((), (), s32[]{:S(2)}) async-start(), calls=%async_computation.8 | async-start | bytes 5242880 | tf_op jit(solution)/shard_map/all_gather | solution.py:53
  26.0 126.8 %all-gather.11.cloned.1.call-start = ((), (), s32[]{:S(2)}) async-start(), calls=%async_computation.9 | async-start | bytes 7077888 | tf_op jit(solution)/shard_map/all_gather | solution.py:152
  27.2 165.6 %all-gather.15.cloned.1.call-start = ((), (), s32[]{:S(2)}) async-start(), calls=%async_computation.11 | async-start | bytes 2359296 | tf_op jit(solution)/shard_map/all_gather | solution.py:153
  28.0 245.1 %all-gather.13.cloned.1.call-start = ((), (), s32[]{:S(2)}) async-start(), calls=%async_computation.10 | async-start | bytes 5242880 | tf_op jit(solution)/shard_map/all_gather | solution.py:53
  30.0 133.9 %copy-start.22 = (f32[1024,64]{0,1:T(8,128)}, f32[1024,64]{0,1:T(8,128)S(1)}, u32[]{:S(2)}) copy-start(f32[1024,64]{0,1:T(8,128)S(1)} %get-tuple-element.49) | copy-start | bytes 786436
  30.0 133.9 %copy-start.24 = (f32[1024,64]{0,1:T(8,128)}, f32[1024,64]{0,1:T(8,128)S(1)}, u32[]{:S(2)}) copy-start(f32[1024,64]{0,1:T(8,128)S(1)} %get-tuple-element.50) | copy-start | bytes 786436
  163.3 21.6 copy-start.16
  165.1 13.2 copy-start.6
  165.1 13.2 copy-start.14
  168.2 5.9 copy-start
  168.2 6.1 copy-start.36
  171.8 6.6 copy-start.42
  181.4 5.8 copy-start.1
  181.4 5.7 copy-start.38
  187.2 3.8 copy-start.44
  191.0 82.1 %copy-start.11 = (bf16[1024,512]{1,0:T(8,128)(2,1)S(1)}, bf16[1024,512]{1,0:T(8,128)(2,1)}, u32[]{:S(2)}) copy-start(bf16[1024,512]{1,0:T(8,128)(2,1)} %param.8) | copy-start | bytes 3145732
  192.2 135.6 %all-gather.23.cloned.1.call-start = ((), (), s32[]{:S(2)}) async-start(), calls=%async_computation.15 | async-start | bytes 9437184 | tf_op jit(solution)/shard_map/all_gather | solution.py:155
  192.7 94.9 %copy-start.46 = (f32[512]{0:T(512)S(1)}, f32[512]{0:T(512)}, u32[]{:S(2)}) copy-start(f32[512]{0:T(512)} %param.14) | copy-start | bytes 6148
  192.8 217.8 %all-gather.17.cloned.1.call-start = ((), (), s32[]{:S(2)}) async-start(), calls=%async_computation.12 | async-start | bytes 5242880 | tf_op jit(solution)/shard_map/all_gather | solution.py:53
  278.4 974.1 %copy-start.10 = (f32[1024,512]{1,0:T(8,128)}, f32[1024,512]{1,0:T(8,128)S(1)}, u32[]{:S(2)}) copy-start(f32[1024,512]{1,0:T(8,128)S(1)} %get-tuple-element.60) | copy-start | bytes 6291460
  278.4 49.4 %copy-start.32 = (bf16[1024,512]{1,0:T(8,128)(2,1)S(1)}, bf16[1024,512]{1,0:T(8,128)(2,1)}, u32[]{:S(2)}) copy-start(bf16[1024,512]{1,0:T(8,128)(2,1)} %param.15) | copy-start | bytes 3145732
  288.9 212.0 %all-gather.19.cloned.1.call-start = ((), (), s32[]{:S(2)}) async-start(), calls=%async_computation.13 | async-start | bytes 18874368 | tf_op jit(solution)/shard_map/all_gather | solution.py:154
  289.7 765.7 %reduce-scatter.9.cloned.1.call-start = ((), (), s32[]{:S(2)}) async-start(), calls=%async_computation.16 | async-start | bytes 41943040 | tf_op jit(solution)/shard_map/reduce_scatter | solution.py:185
  346.1 892.2 %reduce-scatter.11.cloned.1.call-start = ((), (), s32[]{:S(2)}) async-start(), calls=%async_computation.17 | async-start | bytes 10485760 | tf_op jit(solution)/shard_map/reduce_scatter | solution.py:57
  1067.9 3.4 copy-start.21
  1093.0 311.8 %reduce-scatter.13.cloned.1.call-start = ((), (), s32[]{:S(2)}) async-start(), calls=%async_computation.18 | async-start | bytes 10485760 | tf_op jit(solution)/shard_map/reduce_scatter | solution.py:57
  1252.4 3.7 copy-start.26
  1261.8 432.8 %all-gather.21.cloned.1.call-start = ((), (), s32[]{:S(2)}) async-start(), calls=%async_computation.14 | async-start | bytes 20971520 | tf_op jit(solution)/shard_map/all_gather | solution.py:181
  1262.6 639.3 %reduce-scatter.21.cloned.1.call-start = ((), (), s32[]{:S(2)}) async-start(), calls=%async_computation.22 | async-start | bytes 37748736 | tf_op jit(solution)/shard_map/reduce_scatter | solution.py:229
  1288.2 3.0 copy-start.37
  1288.2 3.0 copy-start.43
  1288.2 3.0 copy-start.39
  1288.2 3.0 copy-start.45
  1288.2 760.6 %reduce-scatter.15.cloned.1.call-start = ((), (), s32[]{:S(2)}) async-start(), calls=%async_computation.19 | async-start | bytes 10485760 | tf_op jit(solution)/shard_map/reduce_scatter | solution.py:57
  1291.2 116.7 %copy-start.17 = (bf16[1,1024,512]{1,2,0:T(8,128)(2,1)S(1)}, bf16[1,1024,512]{1,2,0:T(8,128)(2,1)}, u32[]{:S(2)}) copy-start(bf16[1,1024,512]{1,2,0:T(8,128)(2,1)} %copy-done.16) | copy-start | bytes 3145732
  1407.9 16.1 slice-start
  1407.9 16.1 slice-start.1
  1407.9 16.1 slice-start.2
  1407.9 17.9 slice-start.3
  1425.7 8.2 copy-start.15
  1433.9 3.3 copy-start.4
  1437.2 14.9 slice-start.4
  1437.2 14.9 slice-start.5
  1437.2 15.8 slice-start.6
  1437.2 17.1 slice-start.7
  1462.2 5.3 copy-start.2
  1462.2 7.4 copy-start.5
  1470.1 3.5 copy-start.3
  1473.6 2.7 copy-start.31
  1482.7 5.0 copy-start.19
  1482.7 5.0 copy-start.35
  1494.9 11.1 copy-start.18
  1506.0 3.0 copy-start.27
  1506.0 3.0 copy-start.29
  1520.1 625.2 %reduce-scatter.17.cloned.1.call-start = ((), (), s32[]{:S(2)}) async-start(), calls=%async_computation.20 | async-start | bytes 14155776 | tf_op jit(solution)/shard_map/reduce_scatter | solution.py:227
  1533.8 666.6 %reduce-scatter.19.cloned.1.call-start = ((), (), s32[]{:S(2)}) async-start(), calls=%async_computation.21 | async-start | bytes 4718592 | tf_op jit(solution)/shard_map/reduce_scatter | solution.py:228
  1541.8 152.7 %copy-start.33 = (bf16[1024,512]{1,0:T(8,128)(2,1)S(1)}, bf16[1024,512]{1,0:T(8,128)(2,1)}, u32[]{:S(2)}) copy-start(bf16[1024,512]{1,0:T(8,128)(2,1)} %param.15) | copy-start | bytes 3145732
  1541.9 779.0 %reduce-scatter.23.cloned.1.call-start = ((), (), s32[]{:S(2)}) async-start(), calls=%async_computation.23 | async-start | bytes 18874368 | tf_op jit(solution)/shard_map/reduce_scatter | solution.py:230
  1730.9 317.9 %copy-start.12 = (bf16[1024,512]{1,0:T(8,128)(2,1)S(1)}, bf16[1024,512]{1,0:T(8,128)(2,1)}, u32[]{:S(2)}) copy-start(bf16[1024,512]{1,0:T(8,128)(2,1)} %param.8) | copy-start | bytes 3145732
  1730.9 317.9 %copy-start.41 = (f32[1024]{0:T(1024)S(1)}, f32[1024]{0:T(1024)}, u32[]{:S(2)}) copy-start(f32[1024]{0:T(1024)} %copy-done.40) | copy-start | bytes 12292
  1730.9 317.9 %copy-start.47 = (f32[512]{0:T(512)S(1)}, f32[512]{0:T(512)}, u32[]{:S(2)}) copy-start(f32[512]{0:T(512)} %param.13) | copy-start | bytes 6148
  1730.9 320.3 %copy-start.49 = (f32[512]{0:T(512)S(1)}, f32[512]{0:T(512)}, u32[]{:S(2)}) copy-start(f32[512]{0:T(512)} %get-tuple-element.24) | copy-start | bytes 6148
  1730.9 345.9 %copy-start.48 = (f32[1024]{0:T(1024)S(1)}, f32[1024]{0:T(1024)}, u32[]{:S(2)}) copy-start(f32[1024]{0:T(1024)} %get-tuple-element.51) | copy-start | bytes 12292
  (10 other events, 17.1 us)
Sparse Core Ops, SparseCore 0:
  26.1 78.9 all-gather.8
  107.6 45.1 all-gather.10
  154.7 27.8 all-gather.14
  192.3 80.7 all-gather.12
  274.8 52.9 all-gather.22
  329.8 80.7 all-gather.16
  412.5 88.3 all-gather.18
  503.2 552.0 reduce-scatter.8
  1093.1 145.1 reduce-scatter.10
  1261.9 142.8 reduce-scatter.12
  1407.1 287.4 all-gather.20
  1698.4 203.4 reduce-scatter.20
  1904.3 144.4 reduce-scatter.14
  2052.1 93.1 reduce-scatter.16
  2149.1 51.3 reduce-scatter.18
  2204.8 115.9 reduce-scatter.22
where the time goes:
time: 2340 us; the launch traced here: 2330 us
  waiting for transfers between devices  1890 us (81%)
  matrix products  249 us (11%)
  other arithmetic  66.7 us (3%)
  blocking collectives  59.7 us (3%)
  local copies, waits for them, and re-layouts  46.2 us (2%)
    reduce_scatter x1, waiting for transfers between devices, local(): lax.psum_scatter(contract_last(cotangent, shrink_full), 'col', scatter_di...  531 us
    reduce_scatter x3, waiting for transfers between devices, collect(): return lax.psum_scatter(values, 'col', scatter_dimension=1, tiled=True)  400 us
    all_gather x3, waiting for transfers between devices, spread(): return lax.all_gather(values, 'col', axis=1, tiled=True)  219 us
    reduce_scatter x1, waiting for transfers between devices, local(): lax.psum_scatter(expand_grad, 'row', scatter_dimension=1, tiled=True)  171 us
    all_gather x1, waiting for transfers between devices, local(): hidden = lax.all_gather(hidden_local, 'col', axis=1, tiled=True)  153 us
    reduce_scatter x1, waiting for transfers between devices, local(): lax.psum_scatter(shrink_grad, 'row', scatter_dimension=0, tiled=True)  120 us
    all_gather x1, waiting for transfers between devices, local(): lax.all_gather(expand_weight, 'row', axis=1, tiled=True)  90.3 us
    reduce_scatter x1, waiting for transfers between devices, local(): lax.psum_scatter(heads_grad, 'row', scatter_dimension=1, tiled=True)  65 us
  transfers between devices with their start and end apart: 16, of which 15 were waited for; matrix products, arithmetic and copies ran while one was open for 12% of the time, Pallas kernels for 0%

commit v1 on v0

v1 whole, which is shorter than its diff:
```python
import functools

import jax
import jax.numpy as jnp
import numpy as np
from jax import lax
from jax.experimental import pallas as pl
from jax.experimental.pallas import tpu as pltpu
from jax.sharding import PartitionSpec as P

HEAD_DIM = 64
EPSILON = 1e-05
ROPE_BASE = 130000.0
LOW = jnp.bfloat16
WIDE = jnp.float32
LANES = 128
VMEM_LIMIT = 58 * 1024 * 1024


def rotary_tables(length):
    position = np.arange(length, dtype=np.float32)
    inverse = np.power(
        np.float32(ROPE_BASE), -np.arange(0, HEAD_DIM, 2, dtype=np.float32) / np.float32(HEAD_DIM)
    )
    angles = position[:, None] * inverse[None, :]
    angles = np.concatenate([angles] * (2 * LANES // HEAD_DIM), axis=1)
    return (jnp.asarray(np.cos(angles)), jnp.asarray(np.sin(angles)))


def dot(left, right):
    return jnp.dot(left, right, preferred_element_type=WIDE)


def contract_rows(left, right):
    return lax.dot_general(left, right, (((0,), (0,)), ((), ())), preferred_element_type=WIDE)


def contract_last(left, right):
    return lax.dot_general(left, right, (((1,), (1,)), ((), ())), preferred_element_type=WIDE)


def whole_spec(shape):
    return pl.BlockSpec(shape, lambda *_: (0,) * len(shape), pipeline_mode=pl.Buffered(1))


def call(kernel, grid, in_specs, out_specs, out_shape, flops, moved, scratch=()):
    return pl.pallas_call(
        kernel,
        grid=grid,
        in_specs=in_specs,
        out_specs=out_specs,
        out_shape=out_shape,
        scratch_shapes=list(scratch),
        compiler_params=pltpu.CompilerParams(vmem_limit_bytes=VMEM_LIMIT),
        cost_estimate=pl.CostEstimate(flops=int(flops), bytes_accessed=int(moved), transcendentals=0),
    )


def first_half(shape):
    return lax.rem(lax.broadcasted_iota(jnp.int32, shape, 1), HEAD_DIM) < HEAD_DIM // 2


def turn_lanes(values, cosine, sine):
    half = HEAD_DIM // 2
    ahead = pltpu.roll(values, LANES - half, 1)
    behind = pltpu.roll(values, half, 1)
    return values * cosine + jnp.where(first_half(values.shape), -ahead, behind) * sine


def turn_lanes_back(values, cosine, sine):
    half = HEAD_DIM // 2
    spun = values * sine
    ahead = pltpu.roll(spun, LANES - half, 1)
    behind = pltpu.roll(spun, half, 1)
    return values * cosine + jnp.where(first_half(values.shape), ahead, -behind)


def inverse_root(stream):
    return lax.rsqrt(jnp.mean(stream * stream, axis=1, keepdims=True) + EPSILON)


def norm_back(stream, inverse, gain, upstream):
    weighted = gain * upstream
    inner = jnp.sum(weighted * stream, axis=1, keepdims=True)
    return inverse * weighted - inverse * inverse * inverse / stream.shape[1] * stream * inner


def probabilities(query, keys, start):
    tile = query.shape[0]
    square = contract_last(query, keys[start : start + tile])
    below = lax.broadcasted_iota(jnp.int32, square.shape, 0) >= lax.broadcasted_iota(
        jnp.int32, square.shape, 1
    )
    square = jnp.where(below, square, -1e30)
    peak = jnp.max(square, axis=1, keepdims=True)
    if start:
        left = contract_last(query, keys[:start])
        peak = jnp.maximum(peak, jnp.max(left, axis=1, keepdims=True))
        left = jnp.exp(left - peak)
    square = jnp.exp(square - peak)
    sums = jnp.sum(square, axis=1, keepdims=True)
    if start:
        sums = sums + jnp.sum(left, axis=1, keepdims=True)
    scale = 1.0 / sums
    if start:
        return [(0, start, left * scale), (start, start + tile, square * scale)]
    return [(start, start + tile, square * scale)]


def head_lanes(shape, head):
    lane = lax.broadcasted_iota(jnp.int32, shape, 1)
    return (lane >= head * HEAD_DIM) & (lane < (head + 1) * HEAD_DIM)


def pick_head(values, head):
    return jnp.where(head_lanes(values.shape, head), values, jnp.zeros_like(values))


def attend_pair(tile, q_ref, k_ref, v_ref, out_ref, lanes):
    keys, values = k_ref[:, lanes], v_ref[:, lanes]
    for start in range(0, q_ref.shape[0], tile):
        here = slice(start, start + tile)
        total = jnp.zeros((tile, LANES), WIDE)
        for head in range(LANES // HEAD_DIM):
            query = pick_head(q_ref[here, lanes] * (HEAD_DIM**-0.5), head)
            mixed = jnp.zeros((tile, LANES), WIDE)
            for a, b, chances in probabilities(query, keys, start):
                mixed = mixed + dot(chances.astype(LOW), values[a:b])
            total = jnp.where(head_lanes(total.shape, head), mixed, total)
        out_ref[here, lanes] = total.astype(LOW)


def attend_back_pair(
    tile, q_ref, k_ref, v_ref, up_ref, cos_ref, sin_ref, dq_ref, dk_ref, dv_ref, k_sum, v_sum
):
    rows = q_ref.shape[0]
    scale = HEAD_DIM**-0.5
    keys, values = k_ref[...], v_ref[...]
    k_sum[...] = jnp.zeros_like(k_sum)
    v_sum[...] = jnp.zeros_like(v_sum)
    for start in reversed(range(0, rows, tile)):
        here = slice(start, start + tile)
        q_total = jnp.zeros((tile, LANES), WIDE)
        for head in range(LANES // HEAD_DIM):
            query = pick_head(q_ref[here] * scale, head)
            upper = pick_head(up_ref[here], head)
            parts = probabilities(query, keys, start)
            slopes = [contract_last(upper, values[a:b]) for a, b, _ in parts]
            inner = sum(
                jnp.sum(chances * slope, axis=1, keepdims=True)
                for (_, _, chances), slope in zip(parts, slopes)
            )
            for (a, b, chances), slope in zip(parts, slopes):
                v_sum[a:b] += contract_rows(chances.astype(LOW), upper)
                back = (chances * (slope - inner)).astype(LOW)
                k_sum[a:b] += contract_rows(back, query)
                q_total = q_total + dot(back, pick_head(keys[a:b], head))
        q_total = q_total * scale
        dq_ref[here] = turn_lanes_back(q_total, cos_ref[here], sin_ref[here]).astype(LOW)
    for start in range(0, rows, tile):
        here = slice(start, start + tile)
        dk_ref[here] = turn_lanes_back(k_sum[here], cos_ref[here], sin_ref[here]).astype(LOW)
        dv_ref[here] = v_sum[here].astype(LOW)


class Home:
    def __init__(self, n_row, n_col):
        self.n = n = n_col
        self.share = n_row // n
        self.r, self.c = lax.axis_index("row"), lax.axis_index("col")
        owner, b = self.r // self.share, lax.rem(self.r, self.share)
        self.row_to = b * n + self.mix(owner - self.c)
        step = self.unmix(lax.rem(self.r, n))
        self.col_to = lax.rem(self.c + step, n)
        self.col_from = lax.rem(self.c - step + n, n)
        self.row_from = self.col_to * self.share + self.r // n

    def mix(self, step):
        step = lax.rem(step + self.n, self.n)
        return lax.rem(step, 2) * (self.n // 2) + step // 2

    def unmix(self, place):
        return lax.rem(place, self.n // 2) * 2 + place // (self.n // 2)

    def block(self, row):
        step = self.unmix(lax.rem(row, self.n))
        return row // self.n * self.n + lax.rem(self.c - step + self.n, self.n)


MESH = pl.DeviceIdType.MESH
ANY = pl.BlockSpec(memory_space=pl.ANY)


def send(src, dst, send_sem, recv_sem, **device):
    return pltpu.make_async_remote_copy(
        src_ref=src, dst_ref=dst, send_sem=send_sem, recv_sem=recv_sem, device_id=device,
        device_id_type=MESH,
    )


class Pairs:
    def __init__(self, axis, n):
        self.axis, self.n, self.pairs = axis, n, n // 2
        self.me = lax.axis_index(axis)
        self.pair, self.side = self.me // 2, lax.rem(self.me, 2)

    def index(self, step, other=False):
        side = 1 - self.side if other else self.side
        return lax.rem(self.pair + step + self.pairs, self.pairs) * 2 + side

    def to(self, index):
        return {self.axis: index}


class Move:
    def __init__(self, axis, to, src, dst, sems):
        self.away = to != lax.axis_index(axis)
        self.remote = send(src, dst, sems[0], sems[1], **{axis: to})
        self.local = pltpu.make_async_copy(src, dst, sems[2])

    def start(self):
        @pl.when(self.away)
        def _():
            self.remote.start()

        @pl.when(jnp.logical_not(self.away))
        def _():
            self.local.start()

    def finish(self):
        @pl.when(self.away)
        def _():
            self.remote.wait()

        @pl.when(jnp.logical_not(self.away))
        def _():
            self.local.wait()


def move_sems():
    return [pltpu.SemaphoreType.DMA(())] * 3


class PairGather(Pairs):
    def __init__(self, axis, n, own, view, sems):
        super().__init__(axis, n)
        self.own, self.view = own, view
        self.out, self.swap, self.recv, self.local = sems

    def peer(self, s):
        return send(
            self.own, self.view(self.me), self.out.at[s], self.recv.at[self.me],
            **self.to(self.index(s)),
        )

    def arrival(self, s, other):
        index = self.index(-s, other)
        return send(
            self.view(index), self.view(index), self.swap.at[s], self.recv.at[index],
            **self.to(self.index(0, True)),
        )

    def mine(self):
        return send(
            self.own, self.view(self.me), self.swap.at[0], self.recv.at[self.me],
            **self.to(self.index(0, True)),
        )

    def keep(self):
        return pltpu.make_async_copy(self.own, self.view(self.me), self.local)

    def start(self):
        for s in range(1, self.pairs):
            self.peer(s).start()
        self.mine().start()
        self.keep().start()

    def forward(self):
        for s in range(1, self.pairs):
            copy = self.arrival(s, False)
            copy.wait_recv()
            copy.start()

    def arrive(self):
        for s in range(self.pairs):
            self.arrival(s, True).wait_recv()
        self.keep().wait()

    def finish(self):
        for s in range(1, self.pairs):
            self.peer(s).wait_send()
            self.arrival(s, False).wait_send()
        self.mine().wait_send()


def gather_sems(n):
    return [pltpu.SemaphoreType.DMA((n // 2,))] * 2 + [
        pltpu.SemaphoreType.DMA((n,)),
        pltpu.SemaphoreType.DMA(()),
    ]


def tiles(shape, body):
    lead, rows, cols = shape
    step = min(max(65536 // cols, 16), rows)
    per = rows // step

    def run(i, carry):
        body((i // per, pl.ds(pl.multiple_of(lax.rem(i, per) * step, step), step)))
        return carry

    lax.fori_loop(0, lead * per, run, 0)


class PairScatter(Pairs):
    def __init__(self, axis, n, room, sems, source=None):
        super().__init__(axis, n)
        self.away, self.mine, self.swapped, self.got = room
        self.swap_out, self.swap_in, self.out, self.recv = sems[:4]
        self.source = source
        if source is not None:
            self.local = sems[4]

    def swap(self, k):
        source = self.away.at[k] if self.source is None else self.source(k * 2 + 1 - self.side)
        return send(
            source, self.swapped.at[k], self.swap_out.at[k], self.swap_in.at[k],
            **self.to(self.index(0, True)),
        )

    def keep(self, k):
        return pltpu.make_async_copy(
            self.source(k * 2 + self.side), self.mine.at[k], self.local.at[k]
        )

    def start(self):
        for k in range(self.pairs):
            self.swap(k).start()
            self.keep(k).start()

    def peer(self, s):
        index = self.index(s)
        return send(
            self.mine.at[index // 2], self.got.at[s - 1], self.out.at[s - 1], self.recv.at[s - 1],
            **self.to(index),
        )

    def put(self, index, at, value):
        k = index // 2

        @pl.when(lax.rem(index, 2) == self.side)
        def _():
            self.mine[(k,) + at] = value

        @pl.when(lax.rem(index, 2) != self.side)
        def _():
            self.away[(k,) + at] = value

    def pass_on(self, index):
        @pl.when(lax.rem(index, 2) != self.side)
        def _():
            self.swap(index // 2).start()

    def exchange(self, on=True):
        for s in list(range(1, self.pairs)) + [0]:
            k = self.index(s) // 2
            self.swap(k).wait_recv()
            if self.source is not None:
                self.keep(k).wait()

            block = self.mine.shape[1:]

            def add(here):
                at = (k,) + here[3 - len(block) :]
                self.mine[at] = self.mine[at] + self.swapped[at]

            tiles((1,) * (3 - len(block)) + block, add)
            if on and s:
                self.peer(s).start()

    def arrive(self):
        for s in range(1, self.pairs):
            self.peer(s).wait_recv()

    def total(self, here):
        total = self.mine[(self.pair,) + here].astype(WIDE)
        for s in range(1, self.pairs):
            total = total + self.got[(s - 1,) + here].astype(WIDE)
        return total

    def finish(self):
        for k in range(self.pairs):
            self.swap(k).wait_send()
        for s in range(1, self.pairs):
            self.peer(s).wait_send()


def scatter_sems(n, lead=None, source=False):
    pairs = n // 2
    lead = () if lead is None else (lead,)
    sems = [pltpu.SemaphoreType.DMA(lead + (pairs,))] * 2
    sems += [pltpu.SemaphoreType.DMA(lead + (pairs - 1,))] * 2
    return sems + ([pltpu.SemaphoreType.DMA(lead + (pairs,))] if source else [])


def scatter_room(n, block, lead=None, source=False):
    pairs = n // 2
    lead = () if lead is None else (lead,)
    room = [pltpu.VMEM(lead + (pairs,) + block, LOW)] * (2 if source else 3)
    return room + [pltpu.VMEM(lead + (pairs - 1,) + block, LOW)]


def greet(pairs=(), everyone=()):
    barrier = pltpu.get_barrier_semaphore()
    count = 0

    def hello(device):
        pl.semaphore_signal(barrier, inc=1, device_id=device, device_id_type=MESH)

    for axis, n in pairs:
        place = Pairs(axis, n)
        for s in range(1, place.pairs):
            hello(place.to(place.index(s)))
        hello(place.to(place.index(0, True)))
        count += place.pairs
    for axis, n in everyone:
        for s in range(1, n):
            hello({axis: lax.rem(lax.axis_index(axis) + s, n)})
        count += n - 1
    pl.semaphore_wait(barrier, count)


class ColScatter:
    def __init__(self, n, view, own, got, sems):
        self.n, self.view, self.own, self.got = n, view, own, got
        self.out, self.recv, self.local = sems
        self.c = lax.axis_index("col")

    def copy(self, s):
        to = lax.rem(self.c + s, self.n)
        return send(
            self.view(to), self.got.at[s - 1], self.out.at[s - 1], self.recv.at[s - 1], col=to
        )

    def keep(self):
        return pltpu.make_async_copy(self.view(self.c), self.own, self.local)

    def start(self):
        for s in range(1, self.n):
            self.copy(s).start()
        self.keep().start()

    def arrive(self):
        self.keep().wait()
        for s in range(1, self.n):
            self.copy(s).wait_recv()

    def total(self, here):
        total = self.own[here].astype(WIDE)
        for s in range(1, self.n):
            total = total + self.got[(s - 1,) + here].astype(WIDE)
        return total

    def finish(self):
        for s in range(1, self.n):
            self.copy(s).wait_send()


def col_sems(n):
    return [pltpu.SemaphoreType.DMA((n - 1,))] * 2 + [pltpu.SemaphoreType.DMA(())]


def columns(ref, width):
    lead = (slice(None),) * (len(ref.shape) - 1)
    return lambda j: ref.at[lead + (pl.ds(pl.multiple_of(j * width, width), width),)]


def row_blocks(ref, depth):
    return lambda r: ref.at[:, pl.ds(pl.multiple_of(r * depth, depth), depth), :]


def talk(
    kernel, ident, in_specs, out_specs, out_shape, scratch, flops=0, moved=1 << 24, grid=()
):
    return pl.pallas_call(
        kernel,
        grid=grid,
        in_specs=in_specs,
        out_specs=out_specs,
        out_shape=out_shape,
        scratch_shapes=scratch,
        compiler_params=pltpu.CompilerParams(
            vmem_limit_bytes=VMEM_LIMIT, collective_id=ident, has_side_effects=True
        ),
        cost_estimate=pl.CostEstimate(flops=int(flops), bytes_accessed=int(moved), transcendentals=0),
    )


def gather_kernel(n_row, n_col, tokens, gains, heads, merge, shrink, *refs):
    x, gains_full, heads_full, moved, merge_rows, passing = refs[:6]
    sems = list(refs[6:])

    def take(count):
        taken, sems[:] = sems[:count], sems[count:]
        return taken

    width = tokens.shape[1]
    gain_col = PairGather("col", n_col, gains, columns(gains_full, width), take(4))
    merge_col = PairGather("col", n_col, merge, columns(merge_rows, width), take(4))
    x_col = PairGather("col", n_col, tokens, columns(x, width), take(4))
    heads_row = PairGather("row", n_row, heads, row_blocks(heads_full, heads.shape[1]), take(4))
    home = Home(n_row, n_col)
    first_move = Move("row", home.row_to, shrink, passing, take(3))
    second_move = Move("col", home.col_to, passing, moved, take(3))

    greet((), (("row", n_row), ("col", n_col)))
    gain_col.start()
    merge_col.start()
    first_move.start()
    heads_row.start()
    x_col.start()
    gain_col.forward()
    merge_col.forward()
    first_move.finish()
    second_move.start()
    heads_row.forward()
    x_col.forward()
    for job in (heads_row, gain_col, merge_col, x_col):
        job.arrive()
    for job in (heads_row, gain_col, merge_col, x_col, second_move):
        job.finish()


def gather_first(n_row, n_col, tokens, gains, heads, merge, shrink):
    rows, width = tokens.shape
    lead, depth, cols = heads.shape
    merge = merge.reshape((1,) + merge.shape)
    shape = jax.ShapeDtypeStruct
    return talk(
        functools.partial(gather_kernel, n_row, n_col),
        0,
        [ANY] * 5,
        [ANY] * 5,
        [
            shape((rows, width * n_col), LOW),
            shape((gains.shape[0], width * n_col), WIDE),
            shape((lead, depth * n_row, cols), LOW),
            shape(shrink.shape, LOW),
            shape((1, merge.shape[1], width * n_col), LOW),
        ],
        [pltpu.VMEM(shrink.shape, LOW)] + gather_sems(n_col) * 3 + gather_sems(n_row) + move_sems() * 2,
    )(tokens, gains, heads, merge, shrink)


def attend_all_kernel(
    n_row, n_col, steps, x_ref, gain_ref, w_ref, cos_ref, sin_ref, cot, moved, merge_rows,
    normed_ref, q_ref, k_ref, v_ref, cot_full, mixed, spread, merge_full, attended, *sems,
):
    step = pl.program_id(0)
    tile, width = x_ref.shape[0], attended.shape[1]
    half = cot_full.shape[0]
    cot_col = PairGather(
        "col", n_col, cot.at[pl.ds(0, half)], columns(cot_full, width), sems[:4]
    )
    mixed_col = PairGather("col", n_col, attended, columns(mixed, width), sems[4:8])
    home = Home(n_row, n_col)
    shrink_row = PairGather("row", n_row, moved, lambda r: spread.at[home.block(r)], sems[8:12])
    merge_row = PairGather(
        "row", n_row, merge_rows, row_blocks(merge_full, merge_rows.shape[1]), sems[12:16]
    )

    @pl.when(step == 0)
    def _():
        greet((("row", n_row), ("col", n_col)))
        cot_col.start()
        merge_row.start()
        shrink_row.start()

    @pl.when(step < steps)
    def _():
        rows = pl.ds(pl.multiple_of(step * tile, tile), tile)
        stream = x_ref[...].astype(WIDE)
        normed = (stream * inverse_root(stream) * gain_ref[...]).astype(LOW)
        normed_ref[...] = normed
        cosine, sine = cos_ref[rows], sin_ref[rows]
        for p, out in enumerate((q_ref, k_ref, v_ref)):
            projected = dot(normed, w_ref[p])
            for i in range(width // LANES):
                part = projected[:, i * LANES : (i + 1) * LANES]
                if p < 2:
                    part = turn_lanes(part, cosine, sine)
                out[rows, i * LANES : (i + 1) * LANES] = part.astype(LOW)

    @pl.when(step >= steps)
    def _():
        lanes = pl.ds(pl.multiple_of(jnp.maximum(step - steps, 0) * LANES, LANES), LANES)
        attend_pair(tile, q_ref, k_ref, v_ref, attended, lanes)

    @pl.when(step == steps + width // LANES // 2 - 1)
    def _():
        cot_col.forward()

    @pl.when(step == steps + width // LANES - 1)
    def _():
        mixed_col.start()
        merge_row.forward()
        shrink_row.forward()
        mixed_col.forward()
        for job in (merge_row, shrink_row, cot_col, mixed_col):
            job.arrive()
        for job in (merge_row, shrink_row, cot_col, mixed_col):
            job.finish()


def attend_all(n_row, n_col, x, gain, weight, cosine, sine, cot, moved, merge_rows):
    rows, full = x.shape
    width = full // n_col
    tile = min(256, rows)
    steps = rows // tile
    shape = jax.ShapeDtypeStruct
    low = lambda *dims: shape(dims, LOW)
    row = pl.BlockSpec((tile, full), lambda i: (jnp.minimum(i, steps - 1), 0))
    head = whole_spec((rows, width))
    return talk(
        functools.partial(attend_all_kernel, n_row, n_col, steps),
        1,
        [row, whole_spec((1, full)), whole_spec(weight.shape)]
        + [whole_spec((rows, LANES))] * 2
        + [ANY] * 3,
        [row, head, head, head] + [ANY] * 4,
        [low(rows, full)]
        + [low(rows, width)] * 3
        + [low(rows // 2, full), low(rows, full)]
        + [low(n_row, *moved.shape), low(1, merge_rows.shape[1] * n_row, full)],
        [pltpu.VMEM((rows, width), LOW)] + gather_sems(n_col) * 2 + gather_sems(n_row) * 2,
        grid=(steps + width // LANES,),
    )(x, gain, weight, cosine, sine, cot, moved, merge_rows)


def feed_kernel(
    n_row, n_col, steps, x_ref, mixed_ref, merge_ref, gain_ref, w_ref, s_ref, up_ref, cot,
    middle_ref, normed_ref, hidden_ref, gate_ref, upward_ref, grad_ref,
    later, early, *sems,
):
    step = pl.program_id(0)
    tile, full = x_ref.shape
    half = up_ref.shape[0]
    cols = s_ref.shape[3]
    units = hidden_ref.shape[1]
    each = (pl.num_programs(0) - steps) // 2
    cot_col = PairGather(
        "col", n_col, cot.at[pl.ds(half, half)], columns(later, full // n_col), sems
    )
    home = Home(n_row, n_col)

    @pl.when(step == 0)
    def _():
        greet((("col", n_col),))
        cot_col.start()

    @pl.when(step < steps)
    def _():
        rows = pl.ds(pl.multiple_of(jnp.minimum(step, steps - 1) * tile, tile), tile)
        chunk = min(512, full)
        for at in range(0, full, chunk):
            here = slice(at, at + chunk)
            middle_ref[:, here] = x_ref[:, here].astype(WIDE) + dot(
                mixed_ref[...], merge_ref[:, here]
            )

        def norm(i, carry):
            here = pl.ds(pl.multiple_of(i * 32, 32), 32)
            to = pl.ds(pl.multiple_of(jnp.minimum(step, steps - 1) * tile + i * 32, 32), 32)
            middle = middle_ref[here]
            normed_ref[to] = (middle * inverse_root(middle) * gain_ref[...]).astype(LOW)
            return carry

        lax.fori_loop(0, tile // 32, norm, 0)

    @pl.when(step == steps + each // 2)
    def _():
        cot_col.forward()

    @pl.when(step == steps + each)
    def _():
        cot_col.arrive()

    def run(first, upstream):
        block = half
        for start in range(0, half, block):
            here = slice(start, start + block)
            normed = normed_ref[first + start : first + start + block]
            gate = dot(normed, w_ref[0])
            upward = dot(normed, w_ref[1])
            back = sum(
                contract_last(upstream[here, j * cols : (j + 1) * cols], s_ref[0, j])
                for j in range(n_col)
            )
            chance = 1.0 / (1.0 + jnp.exp(-gate))
            active = gate * chance
            hidden_ref[here] = (active * upward).astype(LOW)
            gate_ref[here] = (back * upward * chance * (1.0 + gate * (1.0 - chance))).astype(LOW)
            upward_ref[here] = (back * active).astype(LOW)

    @pl.when((step >= steps) & (step < steps + each))
    def _():
        run(0, up_ref)
        early[jnp.clip(step - steps, 0, each - 1)] = hidden_ref[...]

    @pl.when(step >= steps + each)
    def _():
        run(half, later)
        turned = hidden_ref[...].T
        before = early[jnp.clip(step - steps - each, 0, each - 1)].T
        for j in range(n_col):
            here = slice(j * cols, (j + 1) * cols)
            grad_ref[home.mix(home.c - j)] = (
                dot(before, up_ref[:, here]) + dot(turned, later[:, here])
            ).astype(LOW)

    @pl.when(step == pl.num_programs(0) - 1)
    def _():
        cot_col.finish()


def feed_forward(n_row, n_col, x, mixed, merge, gain, expand, shrink, upstream, cotangent):
    rows, full = x.shape
    units = expand.shape[2]
    share, _, depth, cols = shrink.shape
    half = rows // 2
    tile = min(512, rows)
    steps = rows // tile
    part = min(256, depth)
    each, per = units // part, depth // part
    shape = jax.ShapeDtypeStruct
    row = pl.BlockSpec((tile, full), lambda i: (jnp.minimum(i, steps - 1), 0))
    past = lambda i: jnp.maximum(i - steps, 0)
    unit = lambda i: lax.rem(past(i), each)
    late = lambda i: jnp.maximum(past(i) - each, 0)
    out = pl.BlockSpec((half, part), lambda i: (past(i) // each, unit(i)))
    return talk(
        functools.partial(feed_kernel, n_row, n_col, steps),
        5,
        [
            row,
            row,
            whole_spec(merge.shape),
            whole_spec((1, full)),
            pl.BlockSpec((2, full, part), lambda i: (0, 0, unit(i))),
            pl.BlockSpec((1, n_col, part, cols), lambda i: (unit(i) // per, 0, lax.rem(unit(i), per), 0)),
            whole_spec((half, full)),
            ANY,
        ],
        [
            row,
            whole_spec((rows, full)),
            out,
            out,
            out,
            pl.BlockSpec((n_col, part, cols), lambda i: (late(i) // per, lax.rem(late(i), per), 0)),
        ],
        [shape((rows, full), WIDE), shape((rows, full), LOW)]
        + [shape((rows, units), LOW)] * 3
        + [shape((share * n_col, depth, cols), LOW)],
        [pltpu.VMEM((half, full), LOW), pltpu.VMEM((each, half, part), LOW)] + gather_sems(n_col),
        grid=(steps + 2 * each,),
    )(x, mixed, merge, gain, expand, shrink, upstream, cotangent)


def second_kernel(
    n_row, n_col, steps, gate_ref, upward_ref, w_ref, middle_ref, gain_ref, cot_ref,
    merge_ref, normed_ref, part_ref, grad_ref, out_ref, sum_ref,
    up, away, mine, swapped, got, turned, *sems,
):
    step = pl.program_id(0)
    c = lax.axis_index("col")
    tile, width = cot_ref.shape

    jobs = [
        PairScatter(
            "col", n_col, [ref.at[a] for ref in (away, mine, swapped, got)], [ref.at[a] for ref in sems]
        )
        for a in range(steps)
    ]

    @pl.when(step == 0)
    def _():
        greet((("col", n_col),))
        sum_ref[...] = jnp.zeros_like(sum_ref)

    @pl.when(step < steps)
    def _():
        a = jnp.minimum(step, steps - 1)
        rows = pl.ds(pl.multiple_of(a * tile, tile), tile)
        full = middle_ref.shape[1]
        chunk = min(512, full)
        for at in range(0, full, chunk):
            cols = slice(at, at + chunk)
            up[:, cols] = contract_last(gate_ref[rows], w_ref[0, cols]) + contract_last(
                upward_ref[rows], w_ref[1, cols]
            )

        def norm(i, carry):
            here = pl.ds(pl.multiple_of(i * 32, 32), 32)
            middle, upstream = middle_ref[here], up[here]
            inverse = inverse_root(middle)
            sum_ref[...] += jnp.sum(upstream * (middle * inverse), axis=0, keepdims=True)
            result = norm_back(middle, inverse, gain_ref[...], upstream)
            cotangent = cot_ref[here].astype(WIDE)
            for j in range(n_col):
                mine = (c == j).astype(WIDE)
                part_ref[here, j * width : (j + 1) * width] = (
                    result[:, j * width : (j + 1) * width] + mine * cotangent
                ).astype(LOW)
            return carry

        lax.fori_loop(0, tile // 32, norm, 0)
        for at in range(0, full, chunk):
            cols = slice(at, at + chunk)
            up[:, cols] = contract_last(part_ref[...], merge_ref[cols])
        place = Pairs("col", n_col)
        for j in range(n_col):
            value = up[:, j * width : (j + 1) * width].astype(LOW)

            @pl.when(j % 2 == place.side)
            def _():
                mine[a, j // 2] = value

            @pl.when(j % 2 != place.side)
            def _():
                away[a, j // 2] = value

        for index, job in enumerate(jobs):

            @pl.when(step == index)
            def _():
                for j in range(n_col):
                    job.pass_on(j)

    for index, job in enumerate(jobs):

        @pl.when(step == (index + 2 if index + 2 < steps else steps + 5 * (index + 3 - steps)))
        def _():
            job.exchange()

    @pl.when(step >= steps)
    def _():
        which = lax.rem(step - steps, 2)
        units = gate_ref.shape[1]
        chunk = min(512, units)

        @pl.when(which == 0)
        def _():
            turned[...] = normed_ref[...].T

        for index, ref in enumerate((gate_ref, upward_ref)):

            @pl.when(which == index)
            def _():
                for at in range(0, units, chunk):
                    grad_ref[0, :, at : at + chunk] = dot(
                        turned[...], ref[:, at : at + chunk]
                    ).astype(LOW)

    @pl.when(step == pl.num_programs(0) - 1)
    def _():
        for a, job in enumerate(jobs):
            job.arrive()

            def add(here):
                out_ref[(a,) + here[1:]] = job.total(here[1:]).astype(LOW)

            tiles((1,) + out_ref.shape[1:], add)
        for job in jobs:
            job.finish()


def second_back(n_row, n_col, gate, upward, expand, middle, gain, cotangent, merge, normed):
    rows, full = middle.shape
    units = gate.shape[1]
    width = full // n_col
    tile = min(256, rows)
    steps = rows // tile
    depth = min(256, full)
    later = 2 * (full // depth)
    shape = jax.ShapeDtypeStruct
    row = lambda w: pl.BlockSpec((tile, w), lambda i: (jnp.minimum(i, steps - 1), 0))
    block = (steps, tile, width)
    past = lambda i: jnp.maximum(i - steps, 0)
    outs = talk(
        functools.partial(second_kernel, n_row, n_col, steps),
        2,
        [
            whole_spec((rows, units)),
            whole_spec((rows, units)),
            whole_spec(expand.shape),
            row(full),
            whole_spec((1, full)),
            row(width),
            whole_spec(merge.shape),
            pl.BlockSpec((rows, depth), lambda i: (0, past(i) // 2)),
        ],
        [
            row(full),
            pl.BlockSpec((1, depth, units), lambda i: (lax.rem(past(i), 2), past(i) // 2, 0)),
            whole_spec(block),
            whole_spec((1, full)),
        ],
        [
            shape((rows, full), LOW),
            shape((2, full, units), LOW),
            shape(block, LOW),
            shape((1, full), WIDE),
        ],
        [
            pltpu.VMEM((tile, full), WIDE),
        ]
        + scatter_room(n_col, (tile, width), steps)
        + [pltpu.VMEM((depth, rows), LOW)]
        + scatter_sems(n_col, steps),
        grid=(steps + later,),
    )(gate, upward, expand, middle, gain, cotangent, merge, normed)
    return outs[0], outs[1], outs[2].reshape(rows, width), outs[3]


def attend_back_kernel(
    n_row, n_col, halves, hidden_ref, s_ref, middle, mixed_ref, part_ref,
    q_ref, k_ref, v_ref, up_ref, cos_ref, sin_ref, shrink_sum,
    layer_out, merge_mine, dq_ref, dk_ref, dv_ref, shrink_out, returning,
    merge_away, merge_swap,
    away, mine, swapped, got, middle_own, k_sum, v_sum, middle_sem, back_out, back_in, back_here, *sems,
):
    step = pl.program_id(0)
    home = Home(n_row, n_col)
    back = Move("col", home.col_from, shrink_sum, returning, (back_out, back_in, back_here))
    c = lax.axis_index("col")
    tile, width = layer_out.shape[1:]
    first, second = halves * n_col, halves * n_col + n_row
    jobs = [
        PairScatter(
            "col", n_col, [ref.at[h] for ref in (away, mine, swapped, got)],
            [ref.at[h] for ref in sems[:4]],
        )
        for h in range(halves)
    ]
    place = jobs[0]
    merge_row = PairScatter(
        "row", n_row, (merge_away, merge_mine, merge_swap, None), sems[4:6] + (None, None)
    )

    def middle_copy(h):
        rows = pl.ds(h * tile, tile)
        cols = pl.ds(pl.multiple_of(c * width, width), width)
        return pltpu.make_async_copy(middle.at[rows, cols], middle_own.at[h], middle_sem.at[h])

    @pl.when(step == 0)
    def _():
        greet((("row", n_row),), (("col", n_col),))
        for h in range(halves):
            middle_copy(h).start()

    @pl.when(step == second - 1)
    def _():
        back.start()

    for h, job in enumerate(jobs):

        @pl.when((step >= h * n_col) & (step < (h + 1) * n_col))
        def _():
            at = jnp.clip(step - h * n_col, 0, n_col - 1)
            k = lax.rem(at, place.pairs)
            side = jnp.where(at < place.pairs, 1 - place.side, place.side)
            j = k * 2 + side
            rows = s_ref.shape[2]
            here = slice(h * tile, (h + 1) * tile)
            value = sum(
                dot(hidden_ref[here, i * rows : (i + 1) * rows], s_ref[i, j])
                for i in range(s_ref.shape[0])
            ).astype(LOW)

            @pl.when(at < place.pairs)
            def _():
                job.away[k] = value
                job.swap(k).start()

            @pl.when(at >= place.pairs)
            def _():
                job.mine[k] = value

    @pl.when((step >= first) & (step < second))
    def _():
        row = jnp.clip(step - first, 0, n_row - 1)
        turned = mixed_ref[...].T
        full = part_ref.shape[1]
        chunk = min(512, full)
        for at in range(0, full, chunk):
            merge_row.put(
                row,
                (0, slice(None), slice(at, at + chunk)),
                dot(turned, part_ref[:, at : at + chunk]).astype(LOW),
            )
        merge_row.pass_on(row)

    @pl.when(step >= second)
    def _():
        attend_back_pair(
            min(256, q_ref.shape[0]), q_ref, k_ref, v_ref, up_ref, cos_ref, sin_ref,
            dq_ref, dk_ref, dv_ref, k_sum, v_sum,
        )

    @pl.when(step == second)
    def _():
        merge_row.exchange(False)

    for h, job in enumerate(jobs):

        @pl.when(step == (second - 1 if h == 0 else pl.num_programs(0) - 2))
        def _():
            job.exchange()

    @pl.when(step == pl.num_programs(0) - 1)
    def _():
        for h, job in enumerate(jobs):
            job.arrive()
            middle_copy(h).wait()

            def add(here):
                at = (h,) + here[1:]
                layer_out[at] = (middle_own[at] + job.total(here[1:])).astype(LOW)

            tiles((1, tile, width), add)
        back.finish()
        store = pltpu.make_async_copy(returning, shrink_out, back_here)
        store.start()
        for job in jobs:
            job.finish()
        for k in range(merge_row.pairs):
            merge_row.swap(k).wait_send()
        store.wait()


def attend_back(
    n_row, n_col, hidden, shrink, middle, mixed, part, queries, keys, values, upstream, cosine, sine,
    shrink_sum,
):
    rows, full = middle.shape
    width = full // n_col
    merge_depth = full // n_row
    shape = jax.ShapeDtypeStruct
    halves = 2
    last = halves * n_col + n_row
    pairs = width // LANES
    tile = rows // halves
    block = (halves, tile, width)
    merge_block = (n_row // 2, 1, merge_depth, full)
    merge_row = lambda i: jnp.clip(i - halves * n_col, 0, n_row - 1)
    pair = pl.BlockSpec((rows, LANES), lambda i: (0, jnp.maximum(i - last, 0)))
    table = whole_spec((rows, LANES))
    outs = talk(
        functools.partial(attend_back_kernel, n_row, n_col, halves),
        3,
        [
            whole_spec(hidden.shape),
            whole_spec(shrink.shape),
            ANY,
            pl.BlockSpec((rows, merge_depth), lambda i: (0, merge_row(i))),
            whole_spec(part.shape),
            pair, pair, pair, pair, table, table,
            ANY,
        ],
        [
            whole_spec(block),
            whole_spec(merge_block),
            pair, pair, pair,
            ANY,
        ],
        [shape(block, LOW), shape(merge_block, LOW)]
        + [shape((rows, width), LOW)] * 3
        + [shape(shrink_sum.shape, LOW)],
        [pltpu.VMEM(shrink_sum.shape, LOW)]
        + [pltpu.VMEM(merge_block, LOW)] * 2
        + scatter_room(n_col, (tile, width), halves)
        + [pltpu.VMEM(block, WIDE)]
        + [pltpu.VMEM((rows, LANES), WIDE)] * 2
        + [pltpu.SemaphoreType.DMA((halves,))]
        + move_sems()
        + scatter_sems(n_col, halves)
        + [pltpu.SemaphoreType.DMA((n_row // 2,))] * 2,
        grid=(last + pairs,),
    )(
        hidden, shrink, middle, mixed, part,
        queries, keys, values, upstream, cosine, sine, shrink_sum,
    )
    return outs[0].reshape(rows, width), outs[1], outs[2:5], outs[5]


def finish_kernel(
    n_row, n_col, steps, q_ref, k_ref, v_ref, w_ref, x_ref, gain_ref, part_ref, normed_ref, second_ref,
    merge, returning, tokens_out, heads_out, merge_out, gains_out, shrink_out,
    came, up, away, mine, swapped, got, heads_away, heads_mine, heads_swap, heads_got,
    merge_mine, merge_got, merge_sum, merge_own, merge_cols,
    gains, gains_own, gains_got, gains_all, gains_send, gains_recv, *sems,
):
    step = pl.program_id(0)
    last = pl.num_programs(0) - 1
    r = lax.axis_index("row")
    tile, full = x_ref.shape
    width = full // n_col
    jobs = [
        PairScatter(
            "col", n_col, [ref.at[a] for ref in (away, mine, swapped, got)],
            [ref.at[a] for ref in sems[:4]],
        )
        for a in range(steps)
    ]
    heads_row = PairScatter(
        "row", n_row, (heads_away, heads_mine, heads_swap, heads_got), sems[4:8]
    )
    merge_row = PairScatter(
        "row", n_row, (None, merge, None, merge_got), (None, None) + sems[8:10]
    )
    merge_keep = pltpu.make_async_copy(merge.at[merge_row.pair], merge_mine, sems[10])
    merge_col = ColScatter(n_col, columns(merge_sum, width), merge_own, merge_cols, sems[11:14])
    gains_col = ColScatter(n_col, columns(gains, width), gains_own, gains_got, sems[14:17])
    back = Move("row", Home(n_row, n_col).row_from, returning, came, sems[17:20])

    def spread(s):
        to = lax.rem(r + s, n_row)
        return send(gains_all.at[r], gains_all.at[r], gains_send.at[s - 1], gains_recv.at[r], row=to)

    def gained(s):
        at = lax.rem(r - s + n_row, n_row)
        return send(gains_all.at[at], gains_all.at[at], gains_send.at[s - 1], gains_recv.at[at], row=at)

    @pl.when(step == 0)
    def _():
        greet((), (("row", n_row), ("col", n_col)))
        for s in range(1, merge_row.pairs):
            merge_row.peer(s).start()
        merge_keep.start()
        back.start()
        gains[...] = second_ref[...]

    @pl.when(step < steps)
    def _():
        a = jnp.minimum(step, steps - 1)
        rows = pl.ds(pl.multiple_of(a * tile, tile), tile)
        chunk = min(512, full)
        for at in range(0, full, chunk):
            cols = slice(at, at + chunk)
            up[:, cols] = sum(
                contract_last(ref[rows], w_ref[p, cols]) for p, ref in enumerate((q_ref, k_ref, v_ref))
            )

        def norm(i, carry):
            here = pl.ds(pl.multiple_of(i * 32, 32), 32)
            stream, upstream = x_ref[here].astype(WIDE), up[here]
            inverse = inverse_root(stream)
            gains[0:1] += jnp.sum(upstream * (stream * inverse), axis=0, keepdims=True)
            result = norm_back(stream, inverse, gain_ref[...], upstream)
            up[here] = result + part_ref[here].astype(WIDE)
            return carry

        lax.fori_loop(0, tile // 32, norm, 0)
        place = Pairs("col", n_col)
        for j in range(n_col):
            value = up[:, j * width : (j + 1) * width].astype(LOW)

            @pl.when(j % 2 == place.side)
            def _():
                mine[a, j // 2] = value

            @pl.when(j % 2 != place.side)
            def _():
                away[a, j // 2] = value

        for index, job in enumerate(jobs):

            @pl.when(step == index)
            def _():
                for j in range(n_col):
                    job.pass_on(j)

    @pl.when(step == steps - 1)
    def _():
        gains_col.start()

    @pl.when(step >= steps)
    def _():
        row = jnp.maximum(step - steps, 0)
        turned = normed_ref[...].T
        for p, ref in enumerate((q_ref, k_ref, v_ref)):
            heads_row.put(row, (p,), dot(turned, ref[...]).astype(LOW))
        heads_row.pass_on(row)

    @pl.when(step == last)
    def _():
        heads_row.exchange()
        gains_col.arrive()
        gains_all[r] = gains_col.total((slice(None), slice(None)))
        for s in range(1, n_row):
            spread(s).start()

    for index, job in enumerate(jobs):

        @pl.when(step == (steps + 1 + 3 * index if index < 2 else last))
        def _():
            job.exchange()

    @pl.when(step == last)
    def _():
        merge_row.arrive()
        merge_keep.wait()

        def merge_add(here):
            total = merge_mine[here].astype(WIDE)
            for s in range(1, merge_row.pairs):
                total = total + merge_got[(s - 1,) + here].astype(WIDE)
            merge_sum[here] = total.astype(LOW)

        tiles(merge_sum.shape, merge_add)
        merge_col.start()
        heads_row.arrive()

        def heads_add(here):
            heads_out[here] = heads_row.total(here)

        tiles(heads_out.shape, heads_add)
        back.finish()
        store = pltpu.make_async_copy(came, shrink_out, sems[19])
        store.start()
        for a, job in enumerate(jobs):
            job.arrive()

            def add(here):
                tokens_out[(a,) + here[1:]] = job.total(here[1:])

            tiles((1, tile, width), add)
        for s in range(1, n_row):
            gained(s).wait_recv()
        gains_out[...] = sum(gains_all[i] for i in range(n_row))
        merge_col.arrive()

        def merge_done(here):
            merge_out[here] = merge_col.total(here)

        tiles(merge_out.shape, merge_done)
        for s in range(1, n_row):
            spread(s).wait_send()
        for s in range(1, merge_row.pairs):
            merge_row.peer(s).wait_send()
        for job in jobs + [gains_col, heads_row, merge_col]:
            job.finish()
        store.wait()


def finish(n_row, n_col, ups, weight, x, gain, part, normed, second, merge, returning):
    rows, full = x.shape
    width = full // n_col
    lead = weight.shape[0]
    depth = full // n_row
    tile = min(256, rows)
    steps = rows // tile
    shape = jax.ShapeDtypeStruct
    row = pl.BlockSpec((tile, full), lambda i: (jnp.minimum(i, steps - 1), 0))
    block = (steps, tile, width)
    heads_block = (lead, depth, width)
    merge_block, merge_out = (1, depth, full), (1, depth, width)
    gain_rows = second.shape[0]
    outs = talk(
        functools.partial(finish_kernel, n_row, n_col, steps),
        4,
        [whole_spec((rows, width))] * 3
        + [
            whole_spec(weight.shape),
            row,
            whole_spec((1, full)),
            row,
            pl.BlockSpec((rows, depth), lambda i: (0, jnp.maximum(i - steps, 0))),
            whole_spec(second.shape),
            ANY,
            ANY,
        ],
        [
            whole_spec(block),
            whole_spec(heads_block),
            whole_spec(merge_out),
            whole_spec((gain_rows, width)),
            ANY,
        ],
        [
            shape(block, WIDE),
            shape(heads_block, WIDE),
            shape(merge_out, WIDE),
            shape((gain_rows, width), WIDE),
            shape(returning.shape, LOW),
        ],
        [pltpu.VMEM(returning.shape, LOW), pltpu.VMEM((tile, full), WIDE)]
        + scatter_room(n_col, (tile, width), steps)
        + scatter_room(n_row, heads_block)
        + [
            pltpu.VMEM(merge_block, LOW),
            pltpu.VMEM((n_row // 2 - 1,) + merge_block, LOW),
            pltpu.VMEM(merge_block, LOW),
            pltpu.VMEM(merge_out, LOW),
            pltpu.VMEM((n_col - 1,) + merge_out, LOW),
            pltpu.VMEM((gain_rows, full), WIDE),
            pltpu.VMEM((gain_rows, width), WIDE),
            pltpu.VMEM((n_col - 1, gain_rows, width), WIDE),
            pltpu.VMEM((n_row, gain_rows, width), WIDE),
            pltpu.SemaphoreType.DMA((n_row - 1,)),
            pltpu.SemaphoreType.DMA((n_row,)),
        ]
        + scatter_sems(n_col, steps)
        + scatter_sems(n_row)
        + [pltpu.SemaphoreType.DMA((n_row // 2 - 1,))] * 2
        + [pltpu.SemaphoreType.DMA(())]
        + col_sems(n_col) * 2
        + move_sems(),
        grid=(steps + n_row,),
    )(*ups, weight, x, gain, part, normed, second, merge, returning)
    return outs[0].reshape(rows, width), outs[1], outs[2][0], outs[3], outs[4]


def local(
    tokens,
    heads_weight,
    merge_weight,
    expand_weight,
    shrink_weight,
    first_gain,
    second_gain,
    cotangent,
):
    n_row, n_col = lax.axis_size("row"), lax.axis_size("col")
    length = tokens.shape[0]
    share = n_row // n_col
    shrink_rows, shrink_cols = shrink_weight.shape

    gains = jnp.stack([first_gain, second_gain] + [jnp.zeros_like(first_gain)] * 6)
    x, gains, heads_full, moved, merge_rows = gather_first(
        n_row, n_col, tokens, gains, heads_weight, merge_weight, shrink_weight
    )
    expand_full = lax.all_gather(expand_weight, "row", axis=1, tiled=True)
    first_gains, second_gains = gains[:1], gains[1:2]
    cosine, sine = rotary_tables(length)
    first_normed, queries, keys, values, upstream, mixed, shrink_full, merge_full = attend_all(
        n_row, n_col, x, first_gains, heads_full, cosine, sine, cotangent, moved, merge_rows
    )
    merge_full = merge_full[0]
    shrink_full = shrink_full.reshape(share, n_col, shrink_rows, shrink_cols)
    middle, second_normed, hidden, gate_grad, upward_grad, shrink_blocks = feed_forward(
        n_row, n_col, x, mixed, merge_full, second_gains, expand_full, shrink_full, upstream, cotangent
    )
    shrink_sum = lax.psum_scatter(shrink_blocks, "row", scatter_dimension=0)
    middle_part, expand_grad, mixed_grad, second_sum = second_back(
        n_row, n_col, gate_grad, upward_grad, expand_full, middle, second_gains, cotangent,
        merge_full, second_normed,
    )
    expand_sum = lax.psum_scatter(expand_grad, "row", scatter_dimension=1, tiled=True)
    layer_output, merge_blocks, ups, shrink_sum = attend_back(
        n_row, n_col, hidden, shrink_full, middle, mixed, middle_part,
        queries, keys, values, mixed_grad, cosine, sine, shrink_sum,
    )
    second_rows = jnp.pad(second_sum, ((1, 6), (0, 0)))
    tokens_grad, heads_sum, merge_sum, gain_sums, shrink_sum = finish(
        n_row, n_col, ups, heads_full, x, first_gains, middle_part, first_normed, second_rows,
        merge_blocks, shrink_sum,
    )
    return (
        layer_output,
        tokens_grad,
        heads_sum,
        merge_sum,
        expand_sum.astype(WIDE),
        shrink_sum.astype(WIDE),
        gain_sums[0],
        gain_sums[1],
    )


def solution(mesh):
    in_specs = (
        P("row", "col"),
        P(None, "row", "col"),
        P("row", "col"),
        P(None, "row", "col"),
        P("row", "col"),
        P("col"),
        P("col"),
        P("row", "col"),
    )
    out_specs = (
        P("row", "col"),
        P("row", "col"),
        P(None, "row", "col"),
        P("row", "col"),
        P(None, "row", "col"),
        P("row", "col"),
        P("col"),
        P("col"),
    )
    return jax.shard_map(local, mesh=mesh, in_specs=in_specs, out_specs=out_specs, check_vma=False)
```

time: 2340 us -> 684 us (0.29)
  waiting for transfers between devices: 1890 us -> 0.74 us
  Pallas kernels: 0 us -> 643 us
  matrix products: 249 us -> 0 us
  blocking collectives: 59.7 us -> 0 us
  other arithmetic: 66.7 us -> 8.58 us
  local copies, waits for them, and re-layouts: 46.2 us -> 8.61 us
    reduce_scatter x7 -> x1, waiting for transfers between devices: 1170 us -> 0.01 us  [local(): shrink_sum = lax.psum_scatter(shrink_blocks, 'row', scatter_dimension=0)]
    pallas_call x0 -> x6, Pallas kernels: none -> 643 us  [the longest x1 133 us: attend_all(): talk(functools.partial(attend_all_kernel, n_row, n_col, steps), 1, [row,...]
    all_gather x8 -> x1, waiting for transfers between devices: 548 us -> 0.02 us  [local(): expand_full = lax.all_gather(expand_weight, 'row', axis=1, tiled=True)]
    dot_general x24 -> x0, matrix products: 249 us -> none  [the longest x2 31 us: attention_backward(): jnp.einsum('qhd,khd->hqk', upper, valueset, preferred_element_type=jnp.fl...]
    reduce_scatter x1, waiting for transfers between devices: 171 us -> 0.01 us  [local(): lax.psum_scatter(expand_grad, 'row', scatter_dimension=1, tiled=True)]
    psum x5 -> x0, blocking collectives: 59.7 us -> none  [the longest x4 45.6 us: row_total(): return lax.psum(values, 'col')]
    unnamed x119 -> x14, local copies, waits for them, and re-layouts: 32.2 us -> 4.91 us
  transfers between devices with their start and end apart: 16 -> 3, of which waited for: 15 -> 0; matrix products, arithmetic and copies ran while one was open for 12% -> 1% of each run, Pallas kernels for 0% -> 84%
where the time goes in v1:
time: 684 us; the launch traced here: 675 us
  Pallas kernels  643 us (94%)
  between operations  14.1 us (2%)
  local copies, waits for them, and re-layouts  8.61 us (1%)
  other arithmetic  8.58 us (1%)
    pallas_call x1, Pallas kernels, attend_all(): talk(functools.partial(attend_all_kernel, n_row, n_col, steps), 1, [row,...  133 us
    pallas_call x1, Pallas kernels, finish(): talk(functools.partial(finish_kernel, n_row, n_col, steps), 4, [whole_spe...  113 us
    pallas_call x1, Pallas kernels, gather_first(): talk(functools.partial(gather_kernel, n_row, n_col), 0, [ANY] * 5, [ANY]...  113 us
    pallas_call x1, Pallas kernels, attend_back(): talk(functools.partial(attend_back_kernel, n_row, n_col, halves), 3, [who...  108 us
    pallas_call x1, Pallas kernels, second_back(): talk(functools.partial(second_kernel, n_row, n_col, steps), 2, [whole_spe...  103 us
    pallas_call x1, Pallas kernels, feed_forward(): talk(functools.partial(feed_kernel, n_row, n_col, steps), 5, [row, row, w...  72.9 us
  transfers between devices with their start and end apart: 3, of which 0 were waited for; matrix products, arithmetic and copies ran while one was open for 1% of the time, Pallas kernels for 84%

profile of v1, /device:TPU:0, one launch (start us, length us, event | category | flops | bytes accessed | tf_op | source)
XLA Modules:
  0.0 675.4 jit_solution(15366501002599888945)
XLA Ops:
  7.2 0.0 all-gather.2.cloned.1.call-start
  7.2 0.7 all-gather.2.cloned.1.call-update
  7.9 0.0 reduce-scatter.3.cloned.1.call-start
  8.0 0.1 pad.8.clone
  8.0 0.1 pad.7.clone
  8.1 1.4 maximum_maximum_fusion.gains
  9.5 112.7 %shard_map.161 = (bf16[1024,2048]{1,0:T(8,128)(2,1)}, f32[8,2048]{1,0:T(8,128)}, bf16[3,2048,512]{2,1,0:T(8,128)(2,1)}, bf16[1024,512]{1,0:T(8,128)(2,1)}, bf16[1,256,2048]{2,1,0:T(8,128)(2,1)}) custom-call(bf16[1024,512]{1,0:T(8,128)(2,1)} %tokens.1, f32[8,512]{1,0:T(8,128)} %maximum_maximum_fusion.gains, bf16[3,256,512]{2,1,0:T(8,128)(2,1)} %heads.1, ...), custom_call_target="tpu_custom_call" | custom-call | bytes 16777216 | tf_op jit(solution)/shard_map/pallas_call | solution.py:539
  122.1 1.5 fusion
  123.7 132.8 %shard_map.162 = (bf16[1024,2048]{1,0:T(8,128)(2,1)}, bf16[1024,512]{1,0:T(8,128)(2,1)}, bf16[1024,512]{1,0:T(8,128)(2,1)}, bf16[1024,512]{1,0:T(8,128)(2,1)}, b...) custom-call(bf16[1024,2048]{1,0:T(8,128)(2,1)} %get-tuple-element.42, ...), custom_call_target="tpu_custom_call" | custom-call | bytes 16777216 | tf_op jit(solution)/shard_map/pallas_call | solution.py:624
  256.5 0.0 all-gather.2.cloned.1.call-done.w_ref
  256.5 72.9 %shard_map.163 = (f32[1024,2048]{1,0:T(8,128)}, bf16[1024,2048]{1,0:T(8,128)(2,1)}, bf16[1024,2048]{1,0:T(8,128)(2,1)}, bf16[1024,2048]{1,0:T(8,128)(2,1)}, bf16...) custom-call(bf16[1024,2048]{1,0:T(8,128)(2,1)} %get-tuple-element.42.x_ref, ...), custom_call_target="tpu_custom_call" | custom-call | bytes 16777216 | tf_op jit(solution)/shard_map/pallas_call | solution.py:741
  329.4 0.0 reduce-scatter.3.cloned.1.call-update
  329.4 0.0 reduce-scatter.5.cloned.1.call-start
  329.5 103.5 %shard_map.164 = (bf16[1024,2048]{1,0:T(8,128)(2,1)}, bf16[2,2048,2048]{2,1,0:T(8,128)(2,1)}, bf16[4,256,512]{2,1,0:T(8,128)(2,1)}, f32[1,2048]{1,0:T(1,128)}) custom-call(bf16[1024,2048]{1,0:T(8,128)(2,1)} %get-tuple-element.53.gate_ref, bf16[1024,2048]{1,0:T(8,128)(2,1)} %get-tuple-element.54.upward_ref, ...), custom_call_target="tpu_custom_call" | custom-call | bytes 16777216 | tf_op jit(solution)/shard_map/pallas_call | solution.py:890
  432.9 0.0 copy-start.4
  432.9 0.0 reduce-scatter.5.cloned.1.call-update
  433.0 0.7 copy-done.4
  433.6 0.6 pad.4.second_ref
  434.3 0.0 reduce-scatter.3.cloned.1.call-done
  434.3 108.4 %shard_map.165 = (bf16[2,512,512]{2,1,0:T(8,128)(2,1)}, bf16[4,1,256,2048]{3,2,1,0:T(8,128)(2,1)}, bf16[1024,512]{1,0:T(8,128)(2,1)}, bf16[1024,512]{1,0:T(8,128...) custom-call(bf16[1024,2048]{1,0:T(8,128)(2,1)} %get-tuple-element.51.hidden_ref, ...), custom_call_target="tpu_custom_call" | custom-call | bytes 16777216 | tf_op jit(solution)/shard_map/pallas_call | solution.py:1059
  542.7 113.1 %shard_map.166 = (f32[4,256,512]{2,1,0:T(8,128)}, f32[3,256,512]{2,1,0:T(8,128)}, f32[1,256,512]{2,1,0:T(8,128)}, f32[8,512]{1,0:T(8,128)}, bf16[1024,512]{1,0:T(8,128)(2,1)}) custom-call(bf16[1024,512]{1,0:T(8,128)(2,1)} %get-tuple-element.63.q_ref, bf16[1024,512]{1,0:T(8,128)(2,1)} %get-tuple-element.64.k_ref, bf16[1024,512]{1,0:T(8,128)(2,1)} %get-tuple-element.65.v_ref, ...), custom_call_target="tpu_custom_call" | custom-call | bytes 16777216 | tf_op jit(solution)/shard_map/pallas_call | solution.py:1270
  655.8 0.0 copy-start.2
  655.8 2.9 convert_element_type.9
  658.7 1.4 fusion.1
  660.1 0.0 copy-start
  660.1 0.0 reduce-scatter.5.cloned.1.call-done
  660.1 4.3 convert_element_type.8
  664.4 0.0 copy-start.1
  664.4 0.0 copy-done.2
  664.4 1.0 copy.22
  665.4 0.0 copy-done
  665.4 0.0 copy-start.3
  665.4 1.3 copy.23
  666.7 0.0 copy-done.1
  666.7 1.1 copy.24
  667.8 0.0 copy-done.3
  667.8 0.8 copy.25
  (2 shorter events, 0.0 us)
Async XLA Ops:
  7.2 249.3 %all-gather.2.cloned.1.call-start = ((), (), s32[]{:S(2)}) async-start(), calls=%async_computation.2 | async-start | bytes 18874368 | tf_op jit(solution)/shard_map/all_gather | solution.py:1344
  7.9 426.4 %reduce-scatter.3.cloned.1.call-start = ((), (), s32[]{:S(2)}) async-start(), calls=%async_computation.3 | async-start | bytes 9437184 | tf_op jit(solution)/shard_map/reduce_scatter | solution.py:1355
  329.4 330.7 %reduce-scatter.5.cloned.1.call-start = ((), (), s32[]{:S(2)}) async-start(), calls=%async_computation.4 | async-start | bytes 18874368 | tf_op jit(solution)/shard_map/reduce_scatter | solution.py:1360
  432.9 0.7 copy-start.4
  655.8 8.6 %copy-start.2 = (bf16[2,512,512]{2,1,0:T(8,128)(2,1)S(1)}, bf16[2,512,512]{2,1,0:T(8,128)(2,1)}, u32[]{:S(2)}) copy-start(bf16[2,512,512]{2,1,0:T(8,128)(2,1)} %get-tuple-element.62) | copy-start | bytes 3145732
  660.1 5.3 copy-start
  664.4 2.3 copy-start.1
  665.4 2.5 copy-start.3
Sparse Core Ops, SparseCore 0:
  9.9 153.7 all-gather.1
  329.5 71.4 reduce-scatter.2
  433.1 117.1 reduce-scatter.4
